TPU v7x, 32 devices: a whole 2x2x4 slice. The times are simulated.
32 devices in a mesh: row: 8 (over y, x, core), col: 4 (over z).
Axes of the slice: x: 2, y: 2, z: 4, core: 2. Of those that a mesh axis runs over, the one named last changes fastest.
Arguments:
- users: float32 [8, 2048, 128], P('row', 'col'), may hold values from -2 to 2
- items: float32 [4096, 4, 128], P('row', 'col'), may hold values from -2 to 2
- block_user: int32 [8, 4, 48], P('row', 'col'), may hold values from 0 to 15
- block_item: int32 [8, 4, 48], P('row', 'col'), may hold values from 0 to 31
- ratings: bfloat16 [8, 4, 48, 128, 128], P('row', 'col'), may hold values from 0 to 5
- weights: bfloat16 [8, 4, 48, 128, 128], P('row', 'col'), may hold values from 0.099609375 to 3
Outputs:
- new_users: float32 [8, 2048, 128], P('row', 'col')
- new_items: float32 [4096, 4, 128], P('row', 'col')
All inputs are finite; a program needn't handle non-finite values.
Results may differ from a plain program's by a relative error of at most 0.0021.
Values may be sent and summed in bfloat16 or wider, within the bound.
A program may use at most 64 MiB of HBM per device.

v0:
```python
import jax
import jax.numpy as jnp
from jax import lax
from jax.sharding import PartitionSpec as P

BS = 128


def residuals(ub, vb, rating_tiles, weight_tiles):
    pred = jnp.einsum("bik,bjk->bij", ub, vb, preferred_element_type=jnp.float32)
    wts = weight_tiles.astype(jnp.float32)
    return ((wts * (pred - rating_tiles.astype(jnp.float32))).astype(jnp.bfloat16), wts)


def user_side(resid, wts, vb, bu, slabs):
    ugb = jnp.einsum("bij,bjk->bik", resid, vb, preferred_element_type=jnp.float32)
    uhot = (bu[:, None] == jnp.arange(slabs, dtype=jnp.int32)[None, :]).astype(jnp.float32)
    hi = lax.Precision.HIGHEST
    ugrad = jnp.einsum("bu,bik->uik", uhot, ugb, precision=hi)
    usum = jnp.einsum("bu,bi->ui", uhot, jnp.sum(wts, axis=2), precision=hi)
    return (ugrad.reshape(slabs * BS, -1), usum.reshape(slabs * BS))


def item_side(resid, wts, ub, bi, slabs):
    vgb = jnp.einsum("bij,bik->bjk", resid, ub, preferred_element_type=jnp.float32)
    vhot = (bi[:, None] == jnp.arange(slabs, dtype=jnp.int32)[None, :]).astype(jnp.float32)
    hi = lax.Precision.HIGHEST
    vgrad = jnp.einsum("bv,bjk->vjk", vhot, vgb, precision=hi)
    vsum = jnp.einsum("bv,bj->vj", vhot, jnp.sum(wts, axis=1), precision=hi)
    return (vgrad.reshape(slabs * BS, -1), vsum.reshape(slabs * BS))


def reduce_users(ugrad, usum):
    return (
        lax.psum_scatter(ugrad, "col", scatter_dimension=0, tiled=True),
        lax.psum_scatter(usum, "col", scatter_dimension=0, tiled=True),
    )


def reduce_items(resid, wts, ub, bi, slabs):
    vgrad, vsum = item_side(resid, wts, ub, bi, slabs)
    return (
        lax.psum_scatter(vgrad, "row", scatter_dimension=0, tiled=True),
        lax.psum_scatter(vsum, "row", scatter_dimension=0, tiled=True),
    )


def shards(users, items, block_user, block_item, ratings, weights):
    own_users = users.shape[1]
    own_items = items.shape[0]
    width = users.shape[2]
    user_low = users.reshape(own_users, width).astype(jnp.bfloat16)
    item_low = items.reshape(own_items, width).astype(jnp.bfloat16)
    user_slab = lax.all_gather(user_low, "col", axis=0, tiled=True)
    item_slab = lax.all_gather(item_low, "row", axis=0, tiled=True)
    uslabs = user_slab.shape[0] // BS
    islabs = item_slab.shape[0] // BS
    user_slab = user_slab.reshape(uslabs, BS, width)
    item_slab = item_slab.reshape(islabs, BS, width)
    count = block_user.shape[2]
    bu = block_user.reshape(count)
    bi = block_item.reshape(count)
    rating_tiles = ratings.reshape(count, BS, BS)
    weight_tiles = weights.reshape(count, BS, BS)
    ub = jnp.take(user_slab, bu, axis=0)
    vb = jnp.take(item_slab, bi, axis=0)
    resid, wts = residuals(ub, vb, rating_tiles, weight_tiles)
    ugrad, usum = user_side(resid, wts, vb, bu, uslabs)
    item_total, item_weight = reduce_items(resid, wts, ub, bi, islabs)
    user_total, user_weight = reduce_users(ugrad, usum)
    old_users = users.reshape(own_users, width)
    new_users = old_users - 2.0 * (user_total + 0.5 * old_users) / (1.0 + user_weight[:, None])
    old_items = items.reshape(own_items, width)
    new_items = old_items - 2.0 * (item_total + 0.5 * old_items) / (1.0 + item_weight[:, None])
    return (new_users.reshape(users.shape), new_items.reshape(items.shape))


def solution(mesh):
    return jax.shard_map(
        shards,
        mesh=mesh,
        in_specs=(
            P("row", "col", None),
            P("row", "col", None),
            P("row", "col", None),
            P("row", "col", None),
            P("row", "col", None, None, None),
            P("row", "col", None, None, None),
        ),
        out_specs=(P("row", "col", None), P("row", "col", None)),
        check_vma=False,
    )
```

profile of v0, /device:TPU:0, one launch (start us, length us, event | category | flops | bytes accessed | tf_op | source)
XLA Modules:
  0.0 128.3 jit_solution(11923322755567175663)
XLA Ops:
  7.2 1.6 %convert_element_type.26 = bf16[512,128]{1,0:T(8,128)(2,1)} convert(f32[512,128]{1,0:T(8,128)} %bitcast.65) | non-fusion elementwise | flops 65536 | bytes 393216 | tf_op jit(solution)/shard_map/convert_element_type | solution.py:53
  8.9 0.7 fusion.20
  9.6 1.0 bitcast_convert_fusion
  10.5 17.4 %all_gather.6 = bf16[2048,128]{1,0:T(8,128)(2,1)S(1)} all-gather(bf16[512,128]{1,0:T(8,128)(2,1)S(1)} %bitcast_convert_fusion), channel_id=1, replica_groups=mesh['row'=8,'col'=4] {'col'}, dimensions={0}, use_global_device_ids=true | all-gather | bytes 655360 | tf_op jit(solution)/shard_map/all_gather | solution.py:54
  27.9 0.8 gather_fusion
  28.8 7.9 %all-gather.2.cloned.1.call-done = bf16[4096,128]{1,0:T(8,128)(2,1)} async-done(((bf16[512,128]{1,0:T(8,128)(2,1)}), bf16[4096,128]{1,0:T(8,128)(2,1)}) %all-gather.2.cloned.1.call-update) | async-done | bytes 1048592 | tf_op jit(solution)/shard_map/all_gather | solution.py:55
  36.7 3.2 %gather_fusion.1 = bf16[48,128,128]{2,1,0:T(8,128)(2,1)} fusion(bf16[32,128,128]{2,1,0:T(8,128)(2,1)} %bitcast.64, s32[1024]{0:T(1024)S(1)} %pad_clamp_fusion), kind=kCustom, calls=%fused_computation.1 | custom fusion | bytes 3145920 | tf_op jit(solution)/shard_map/jit(_take)/gather | solution.py:66
  39.9 3.8 %fusion.1 = bf16[48,128,128]{2,1,0:T(8,128)(2,1)S(1)} fusion(bf16[1,1,48,128,128]{4,3,2,1,0:T(8,128)(2,1)} %param.11, bf16[1,1,48,128,128]{4,3,2,1,0:T(8,128)(2,1)} %param.10, bf16[48,128,128]{2,1,0:T(8,128)(2,1)S(1)} %gather_fusion, pred[48]{0:T(512)(128)(4,1)S(1)} %compare_and_fusion.1, bf16[48,128,128]{2,1,0:T(8,128)(2,1)} %gather_fusion.1, ...), kind=kOutput, calls=%fused_computation.6 | convolution fusion | flops 206831616 | bytes 7864416 | tf_op jit(solution)/shard_map/bik,bjk->bij/dot_general | solution.py:10
  43.6 0.6 fusion.7
  44.3 2.9 %fusion.4 = f32[16,128,128]{2,0,1:T(8,128)S(1)} fusion(f32[48,128,128]{2,1,0:T(8,128)S(1)} %fusion.7, s32[48]{0:T(128)S(1)} %bitcast.68), kind=kOutput, calls=%fused_computation.10 | convolution fusion | flops 150995712 | bytes 4194496 | tf_op jit(solution)/shard_map/bu,bik->uik/dot_general | solution.py:19
  47.2 1.3 %copy.12 = f32[16,128,128]{2,1,0:T(8,128)} copy(f32[16,128,128]{2,0,1:T(8,128)S(1)} %fusion.4) | data formatting | bytes 2097152 | tf_op jit(solution)/shard_map/bu,bik->uik/dot_general | solution.py:19
  48.6 0.2 reduce-scatter.5.cloned.1.call-start
  48.8 0.8 fusion.6
  49.6 3.2 %fusion.2 = f32[32,128,128]{2,0,1:T(8,128)S(1)} fusion(f32[48,128,128]{2,1,0:T(8,128)S(1)} %fusion.6, s32[48]{0:T(128)S(1)} %bitcast.70), kind=kOutput, calls=%fused_computation.8 | convolution fusion | flops 301991424 | bytes 5243072 | tf_op jit(solution)/shard_map/bv,bjk->vjk/dot_general | solution.py:28
  52.8 2.6 %copy.15 = f32[32,128,128]{2,1,0:T(8,128)} copy(f32[32,128,128]{2,0,1:T(8,128)S(1)} %fusion.2) | data formatting | bytes 4194304 | tf_op jit(solution)/shard_map/bv,bjk->vjk/dot_general | solution.py:28
  55.4 0.6 copy-done.7
  56.0 0.6 dynamic-slice
  56.6 0.6 dynamic-slice.2
  58.5 0.5 convert_reduce_fusion
  59.2 12.5 %all-reduce = f32[2048]{0:T(1024)S(1)} all-reduce(f32[2048]{0:T(1024)S(1)} %convolution_bitcast_fusion.1), channel_id=3, replica_groups=mesh['row'=8,'col'=4] {'col'}, use_global_device_ids=true, to_apply=%region_2.3.clone | all-reduce | flops 2048 | bytes 16384
  71.8 22.7 %all-reduce.1 = f32[4096]{0:T(1024)S(1)} all-reduce(f32[4096]{0:T(1024)S(1)} %convolution_bitcast_fusion), channel_id=5, replica_groups=mesh['row'=8,'col'=4] {'row'}, use_global_device_ids=true, to_apply=%region_5.6.clone | all-reduce | flops 4096 | bytes 32768
  94.7 1.8 %fusion.11 = f32[1,512,128]{2,1,0:T(8,128)} fusion(f32[512,128]{1,0:T(8,128)} %reduce-scatter.3.cloned.1.call-done, f32[1,512,128]{2,1,0:T(8,128)S(1)} %copy-done.2, f32[512]{0:T(512)S(1)} %dynamic-slice_add_fusion.1), kind=kLoop, calls=%fused_computation.24 | loop fusion | flops 327680 | bytes 788480 | tf_op jit(solution)/shard_map/reshape | solution.py:75
  96.5 23.5 %reduce-scatter.5.cloned.1.call-done = f32[512,128]{1,0:T(8,128)} async-done(((f32[4096,128]{1,0:T(8,128)}), f32[512,128]{1,0:T(8,128)}) %reduce-scatter.5.cloned.1.call-update) | async-done | bytes 262160 | tf_op jit(solution)/shard_map/reduce_scatter | solution.py:43
  120.0 1.8 %divide_subtract_fusion = f32[512,128]{1,0:T(8,128)} fusion(f32[512,128]{1,0:T(8,128)S(1)} %bitcast.66, f32[512,128]{1,0:T(8,128)} %reduce-scatter.5.cloned.1.call-done, f32[512]{0:T(512)S(1)} %dynamic-slice_add_fusion), kind=kLoop, calls=%fused_computation.25 | loop fusion | flops 327680 | bytes 788480 | tf_op jit(solution)/shard_map/sub | solution.py:74
  (30 shorter events, 0.6 us)
Async XLA Ops:
  7.2 29.5 %all-gather.2.cloned.1.call-start = ((), (), s32[]{:S(2)}) async-start(), calls=%async_computation.2 | async-start | bytes 1179648 | tf_op jit(solution)/shard_map/all_gather | solution.py:55
  8.9 85.8 %reduce-scatter.3.cloned.1.call-start = ((), (), s32[]{:S(2)}) async-start(), calls=%async_computation.3 | async-start | bytes 1310720 | tf_op jit(solution)/shard_map/reduce_scatter | solution.py:35
  27.9 0.9 copy-start.5
  27.9 0.9 copy-start.4
  39.9 3.8 %copy-start = (bf16[48,128,128]{2,1,0:T(8,128)(2,1)S(1)}, bf16[48,128,128]{2,1,0:T(8,128)(2,1)}, u32[]{:S(2)}) copy-start(bf16[48,128,128]{2,1,0:T(8,128)(2,1)} %gather_fusion.1) | copy-start | bytes 4718596
  48.6 71.4 %reduce-scatter.5.cloned.1.call-start = ((), (), s32[]{:S(2)}) async-start(), calls=%async_computation.4 | async-start | bytes 2359296 | tf_op jit(solution)/shard_map/reduce_scatter | solution.py:43
  55.4 0.7 copy-start.7
  55.4 1.2 copy-start.6
  55.4 3.1 %copy-start.1 = (bf16[1,1,48,128,128]{4,3,2,1,0:T(8,128)(2,1)S(1)}, bf16[1,1,48,128,128]{4,3,2,1,0:T(8,128)(2,1)}, u32[]{:S(2)}) copy-start(bf16[1,1,48,128,128]{4,3,2,1,0:T(8,128)(2,1)} %param.11) | copy-start | bytes 4718596
  55.4 39.3 %copy-start.2 = (f32[1,512,128]{2,1,0:T(8,128)S(1)}, f32[1,512,128]{2,1,0:T(8,128)}, u32[]{:S(2)}) copy-start(f32[1,512,128]{2,1,0:T(8,128)} %param.6) | copy-start | bytes 786436
  55.4 64.6 %copy-start.3 = (f32[512,1,128]{2,1,0:T(1,128)S(1)}, f32[512,1,128]{2,1,0:T(1,128)}, u32[]{:S(2)}) copy-start(f32[512,1,128]{2,1,0:T(1,128)} %param.7) | copy-start | bytes 786436
Sparse Core Ops, SparseCore 0:
  10.5 26.1 all-gather.1
  48.7 27.6 reduce-scatter.2
  80.0 39.8 reduce-scatter.4
where the time goes:
time: 129 us; the launch traced here: 128 us
  blocking collectives  52.6 us (41%)
  waiting for transfers between devices  31.4 us (24%)
  between operations  15.2 us (12%)
  matrix products  11.6 us (9%)
  local copies, waits for them, and re-layouts  9.71 us (8%)
  other arithmetic  7.52 us (6%)
    unnamed x2, blocking collectives  35.2 us
    reduce_scatter x1, waiting for transfers between devices, reduce_items(): lax.psum_scatter(vgrad, 'row', scatter_dimension=0, tiled=True)  23.5 us
    all_gather x1, blocking collectives, shards(): user_slab = lax.all_gather(user_low, 'col', axis=0, tiled=True)  17.4 us
    all_gather x1, waiting for transfers between devices, shards(): item_slab = lax.all_gather(item_low, 'row', axis=0, tiled=True)  7.85 us
    dot_general x1, matrix products, residuals(): jnp.einsum('bik,bjk->bij', ub, vb, preferred_element_type=jnp.float32)  3.76 us
    dot_general x1, matrix products, item_side(): vgrad = jnp.einsum('bv,bjk->vjk', vhot, vgb, precision=hi)  3.25 us
    gather x1, local copies, waits for them, and re-layouts, shards(): vb = jnp.take(item_slab, bi, axis=0)  3.18 us
    dot_general x1, matrix products, user_side(): ugrad = jnp.einsum('bu,bik->uik', uhot, ugb, precision=hi)  2.93 us
  transfers between devices with their start and end apart: 3, of which 2 were waited for; matrix products, arithmetic and copies ran while one was open for 10% of the time, Pallas kernels for 0%

commit v1 on v0

v1 whole, which is shorter than its diff:
```python
import functools

import jax
import jax.numpy as jnp
from jax import lax
from jax.experimental import pallas as pl
from jax.experimental.pallas import tpu as pltpu
from jax.sharding import PartitionSpec as P

BS = 128
MESH = pl.DeviceIdType.MESH
NT = (((1,), (1,)), ((), ()))
NN = (((1,), (0,)), ((), ()))
TN = (((0,), (0,)), ((), ()))


def dot(a, b, dims):
    return lax.dot_general(a, b, dims, preferred_element_type=jnp.float32)


def chain_tables(key_ref, pad_ref, count):
    pad_ref[...] = jnp.full((8, 128), -1, jnp.int32)
    pad_ref[0:1, 0:count] = key_ref[...]
    across = jnp.broadcast_to(pad_ref[0:1, :], (128, 128))
    down = across.T
    i = lax.broadcasted_iota(jnp.int32, (128, 128), 0)
    j = lax.broadcasted_iota(jnp.int32, (128, 128), 1)
    prev = jnp.max(jnp.where((down == across) & (i < j), i + 1, 0), axis=0, keepdims=True)
    last = jnp.max(jnp.where(down == j, i + 1, 0), axis=0, keepdims=True)
    return prev, last, jnp.maximum(pad_ref[0:1, :], 0)


def spots(index, own):
    if own >= BS:
        blocks = own // BS
        return [(index * blocks + k, 0, BS) for k in range(blocks)]
    per = BS // own
    return [(lax.div(index, per), lax.rem(index, per) * own, own)]


def part(block, first, rows, turn_ref):
    if rows == BS:
        return block
    turn_ref[...] = block
    return turn_ref[pl.ds(pl.multiple_of(first, rows), rows), :]


def owned(slab_ref, index, own):
    if own >= BS:
        return slab_ref.at[pl.ds(index * (own // BS), own // BS)]
    per = BS // own
    return slab_ref.at[lax.div(index, per), pl.ds(pl.multiple_of(lax.rem(index, per) * own, own), own)]


def weight_tile(wseg_ref, slots):
    row = lax.broadcasted_iota(jnp.int32, (8, 128), 0)
    tile = jnp.zeros((8, 128), jnp.float32)
    for k, slot in enumerate(slots):
        tile = jnp.where(row == k, wseg_ref[slot], tile)
    return tile


def pack(seg_ref, wseg_ref, tab, line, index, own, out_ref, place, turn_ref):
    pieces = spots(index, own)
    slots = [tab[line, block] for block, _, _ in pieces]
    for k, (slot, (_, first, rows)) in enumerate(zip(slots, pieces)):
        out_ref[place, k * BS : k * BS + rows, :] = part(seg_ref[slot], first, rows, turn_ref).astype(jnp.bfloat16)
    tile = weight_tile(wseg_ref, slots)
    high = tile.astype(jnp.bfloat16).astype(jnp.float32)
    both = jnp.concatenate([high, tile - high], axis=0)
    out_ref[place, own : own + 16, :] = both.astype(jnp.bfloat16)


def update(old_ref, seg_ref, wseg_ref, tab, line, index, own, recv_ref, waits, acc_ref, turn_ref, new_ref):
    pieces = spots(index, own)
    slots = [tab[line, block] for block, _, _ in pieces]
    for k, (slot, (_, first, rows)) in enumerate(zip(slots, pieces)):
        acc_ref[k * BS : k * BS + rows, :] = part(seg_ref[slot], first, rows, turn_ref)
    tile = weight_tile(wseg_ref, slots)
    for place, wait in enumerate(waits):
        wait()
        acc_ref[...] += recv_ref[place, 0:own, :].astype(jnp.float32)
        both = recv_ref[place, own : own + 16, :].astype(jnp.float32)
        tile = tile + (both[0:8] + both[8:16])
    for k, (_, first, rows) in enumerate(pieces):
        turned = jnp.broadcast_to(tile[k : k + 1, :], (BS, BS)).T
        turned = part(turned, first, rows, turn_ref)
        at = slice(k * BS, k * BS + rows)
        old = old_ref[at, :]
        new_ref[at, :] = old - 2.0 * (acc_ref[at, :] + 0.5 * old) / (1.0 + turned)


def kernel(
    n_row, n_col, count, own_u, own_i,
    users, items, bu, bi, ratings, weights,
    new_users, new_items,
    slab_u, slab_i, rat, wts, resid, seg_u, seg_i, wseg_u, wseg_i,
    send_u, send_i, recv_u, recv_i, acc_u, acc_i, turn, pad, tab_v, tab,
    load_sem, gu_send, gu_recv, gi_send, gi_recv, ru_send, ru_recv, ri_send, ri_recv,
):
    row, col = lax.axis_index("row"), lax.axis_index("col")
    col_peers = [lax.rem(col + d, n_col) for d in range(1, n_col)]
    row_peers = [lax.rem(row + d, n_row) for d in range(1, n_row)]

    barrier = pltpu.get_barrier_semaphore()
    for peer in col_peers:
        pl.semaphore_signal(barrier, inc=1, device_id=(row, peer), device_id_type=MESH)
    for peer in row_peers:
        pl.semaphore_signal(barrier, inc=1, device_id=(peer, col), device_id_type=MESH)
    load_rat = pltpu.make_async_copy(ratings, rat, load_sem.at[0])
    load_wts = pltpu.make_async_copy(weights, wts, load_sem.at[1])
    load_rat.start()
    load_wts.start()
    mine_u, mine_i = owned(slab_u, col, own_u), owned(slab_i, row, own_i)
    mine_u[...] = users[...].astype(jnp.bfloat16).reshape(mine_u.shape)
    mine_i[...] = items[...].astype(jnp.bfloat16).reshape(mine_i.shape)
    pl.semaphore_wait(barrier, n_col + n_row - 2)

    gathers = []
    for place, peer in enumerate(col_peers):
        gathers.append(pltpu.make_async_remote_copy(
            src_ref=mine_u, dst_ref=mine_u,
            send_sem=gu_send.at[place], recv_sem=gu_recv.at[place],
            device_id=(row, peer), device_id_type=MESH))
    for place, peer in enumerate(row_peers):
        gathers.append(pltpu.make_async_remote_copy(
            src_ref=mine_i, dst_ref=mine_i,
            send_sem=gi_send.at[place], recv_sem=gi_recv.at[place],
            device_id=(peer, col), device_id_type=MESH))
    for copy in gathers:
        copy.start()

    prev_u, last_u, key_u = chain_tables(bu, pad, count)
    prev_i, last_i, key_i = chain_tables(bi, pad, count)
    for line, values in enumerate((prev_u, prev_i, last_u, last_i, key_u, key_i)):
        tab_v[line : line + 1, :] = values
    to_scalar = pltpu.make_async_copy(tab_v, tab, load_sem.at[2])
    to_scalar.start()
    seg_u[0] = jnp.zeros((BS, BS), jnp.float32)
    seg_i[0] = jnp.zeros((BS, BS), jnp.float32)
    wseg_u[0] = jnp.zeros((8, BS), jnp.float32)
    wseg_i[0] = jnp.zeros((8, BS), jnp.float32)
    to_scalar.wait()
    load_rat.wait()
    load_wts.wait()

    ones = jnp.ones((8, BS), jnp.bfloat16)

    def weight_step(b, carry):
        w = wts[b]
        wseg_u[b + 1] = wseg_u[tab[0, b]] + dot(ones, w, NT)
        wseg_i[b + 1] = wseg_i[tab[1, b]] + dot(ones, w, NN)
        return carry

    lax.fori_loop(0, count, weight_step, 0, unroll=4)

    for copy in gathers:
        copy.wait()

    def user_step(b, carry):
        u = slab_u[tab[4, b]]
        v = slab_i[tab[5, b]]
        pred = dot(u, v, NT)
        r = (wts[b].astype(jnp.float32) * (pred - rat[b].astype(jnp.float32))).astype(jnp.bfloat16)
        resid[b] = r
        seg_u[b + 1] = seg_u[tab[0, b]] + dot(r, v, NN)
        return carry

    lax.fori_loop(0, count, user_step, 0, unroll=4)

    sends_u = []
    for place, peer in enumerate(col_peers):
        pack(seg_u, wseg_u, tab, 2, peer, own_u, send_u, place, turn)
        copy = pltpu.make_async_remote_copy(
            src_ref=send_u.at[place], dst_ref=recv_u.at[place],
            send_sem=ru_send.at[place], recv_sem=ru_recv.at[place],
            device_id=(row, peer), device_id_type=MESH)
        copy.start()
        sends_u.append(copy)

    def item_step(b, carry):
        u = slab_u[tab[4, b]]
        seg_i[b + 1] = seg_i[tab[1, b]] + dot(resid[b], u, TN)
        return carry

    lax.fori_loop(0, count, item_step, 0, unroll=4)

    sends_i = []
    for place, peer in enumerate(row_peers):
        pack(seg_i, wseg_i, tab, 3, peer, own_i, send_i, place, turn)
        copy = pltpu.make_async_remote_copy(
            src_ref=send_i.at[place], dst_ref=recv_i.at[place],
            send_sem=ri_send.at[place], recv_sem=ri_recv.at[place],
            device_id=(peer, col), device_id_type=MESH)
        copy.start()
        sends_i.append(copy)

    update(users, seg_u, wseg_u, tab, 2, col, own_u, recv_u, [c.wait_recv for c in sends_u], acc_u, turn, new_users)
    update(items, seg_i, wseg_i, tab, 3, row, own_i, recv_i, [c.wait_recv for c in sends_i], acc_i, turn, new_items)
    for copy in sends_u + sends_i:
        copy.wait_send()


def shards(n_row, n_col, users, items, block_user, block_item, ratings, weights):
    own_u, own_i = users.shape[1], items.shape[0]
    width = users.shape[2]
    count = block_user.shape[2]
    all_u, all_i = own_u * n_col, own_i * n_row
    vmem = pl.BlockSpec(memory_space=pltpu.VMEM)
    hbm = pl.BlockSpec(memory_space=pl.ANY)
    bf16, f32, i32 = jnp.bfloat16, jnp.float32, jnp.int32
    dma = pltpu.SemaphoreType.DMA
    new_users, new_items = pl.pallas_call(
        functools.partial(kernel, n_row, n_col, count, own_u, own_i),
        out_shape=(
            jax.ShapeDtypeStruct((own_u, width), f32),
            jax.ShapeDtypeStruct((own_i, width), f32),
        ),
        in_specs=[vmem, vmem, vmem, vmem, hbm, hbm],
        out_specs=(vmem, vmem),
        scratch_shapes=[
            pltpu.VMEM((all_u // BS, BS, width), bf16),
            pltpu.VMEM((all_i // BS, BS, width), bf16),
            pltpu.VMEM((count, BS, BS), bf16),
            pltpu.VMEM((count, BS, BS), bf16),
            pltpu.VMEM((count, BS, BS), bf16),
            pltpu.VMEM((count + 1, BS, width), f32),
            pltpu.VMEM((count + 1, BS, width), f32),
            pltpu.VMEM((count + 1, 8, BS), f32),
            pltpu.VMEM((count + 1, 8, BS), f32),
            pltpu.VMEM((n_col - 1, own_u + 16, width), bf16),
            pltpu.VMEM((n_row - 1, own_i + 16, width), bf16),
            pltpu.VMEM((n_col - 1, own_u + 16, width), bf16),
            pltpu.VMEM((n_row - 1, own_i + 16, width), bf16),
            pltpu.VMEM((own_u, width), f32),
            pltpu.VMEM((own_i, width), f32),
            pltpu.VMEM((BS, BS), f32),
            pltpu.VMEM((8, 128), i32),
            pltpu.VMEM((8, 128), i32),
            pltpu.SMEM((8, 128), i32),
            dma((3,)),
            dma((n_col - 1,)),
            dma((n_col - 1,)),
            dma((n_row - 1,)),
            dma((n_row - 1,)),
            dma((n_col - 1,)),
            dma((n_col - 1,)),
            dma((n_row - 1,)),
            dma((n_row - 1,)),
        ],
        compiler_params=pltpu.CompilerParams(
            collective_id=0, has_side_effects=True, vmem_limit_bytes=40 << 20
        ),
        cost_estimate=pl.CostEstimate(
            flops=6 * count * BS * BS * width, bytes_accessed=4 * count * BS * BS, transcendentals=0
        ),
    )(
        users.reshape(own_u, width),
        items.reshape(own_i, width),
        block_user.reshape(1, count),
        block_item.reshape(1, count),
        ratings.reshape(count, BS, BS),
        weights.reshape(count, BS, BS),
    )
    return (new_users.reshape(users.shape), new_items.reshape(items.shape))


def solution(mesh):
    sizes = dict(mesh.shape)
    return jax.shard_map(
        functools.partial(shards, sizes["row"], sizes["col"]),
        mesh=mesh,
        in_specs=(
            P("row", "col", None),
            P("row", "col", None),
            P("row", "col", None),
            P("row", "col", None),
            P("row", "col", None, None, None),
            P("row", "col", None, None, None),
        ),
        out_specs=(P("row", "col", None), P("row", "col", None)),
        check_vma=False,
    )
```

time: 129 us -> 51.3 us (0.40)
  the two profiles are of different devices: /device:TPU:0 before, /device:TPU:1 now
where the time goes in v1:
time: 51.3 us; the launch traced here: 51 us
  Pallas kernels  43 us (84%)
  local copies, waits for them, and re-layouts  7.42 us (14%)
  between operations  0.65 us (1%)
    pallas_call x1, Pallas kernels, shards(): pl.pallas_call(functools.partial(kernel, n_row, n_col, count, own_u, own_...  43 us
    unnamed x14, local copies, waits for them, and re-layouts  7.42 us

profile of v1, /device:TPU:1, one launch (start us, length us, event | category | flops | bytes accessed | tf_op | source)
XLA Modules:
  0.0 51.0 jit_solution(10641608808900619558)
XLA Ops:
  0.6 0.0 copy-start
  0.6 1.4 %copy-done = bf16[1,1,48,128,128]{4,3,2,1,0:T(8,128)(2,1)S(1)} copy-done((bf16[1,1,48,128,128]{4,3,2,1,0:T(8,128)(2,1)S(1)}, bf16[1,1,48,128,128]{4,3,2,1,0:T(8,128)(2,1)}, u32[]{:S(2)}) %copy-start) | copy-done | bytes 1572888
  2.0 0.0 copy-start.1
  2.0 1.4 %copy-done.1 = bf16[1,1,48,128,128]{4,3,2,1,0:T(8,128)(2,1)S(1)} copy-done((bf16[1,1,48,128,128]{4,3,2,1,0:T(8,128)(2,1)S(1)}, bf16[1,1,48,128,128]{4,3,2,1,0:T(8,128)(2,1)}, u32[]{:S(2)}) %copy-start.1) | copy-done | bytes 1572888
  3.4 0.0 copy-start.2
  3.5 0.9 %copy-done.2 = f32[1,512,128]{2,1,0:T(8,128)S(1)} copy-done((f32[1,512,128]{2,1,0:T(8,128)S(1)}, f32[1,512,128]{2,1,0:T(8,128)}, u32[]{:S(2)}) %copy-start.2) | copy-done | bytes 262168
  4.4 0.0 copy-start.3
  4.4 0.9 %copy-done.3 = f32[512,1,128]{2,1,0:T(1,128)S(1)} copy-done((f32[512,1,128]{2,1,0:T(1,128)S(1)}, f32[512,1,128]{2,1,0:T(1,128)}, u32[]{:S(2)}) %copy-start.3) | copy-done | bytes 262168
  5.3 0.0 copy-start.4
  5.4 0.7 %copy-done.4 = s32[1,1,48]{2,1,0:T(1,128)S(1)} copy-done((s32[1,1,48]{2,1,0:T(1,128)S(1)}, s32[1,1,48]{2,1,0:T(1,128)}, u32[]{:S(2)}) %copy-start.4) | copy-done | bytes 216
  6.0 0.0 copy-start.5
  6.0 0.7 %copy-done.5 = s32[1,1,48]{2,1,0:T(1,128)S(1)} copy-done((s32[1,1,48]{2,1,0:T(1,128)S(1)}, s32[1,1,48]{2,1,0:T(1,128)}, u32[]{:S(2)}) %copy-start.5) | copy-done | bytes 216
  6.7 43.0 %shard_map.77 = (f32[512,128]{1,0:T(8,128)S(1)}, f32[512,128]{1,0:T(8,128)S(1)}) custom-call(f32[512,128]{1,0:T(8,128)S(1)} %bitcast.14, f32[512,128]{1,0:T(8,128)S(1)} %bitcast.15, s32[1,48]{1,0:T(1,128)S(1)} %bitcast.16, s32[1,48]{1,0:T(1,128)S(1)} %bitcast.17, bf16[48,128,128]{2,1,0:T(8,128)(2,1)S(1)} %bitcast.10, bf16[48,128,128]{2,1,0:T(8,128)(2,1)S(1)} %bitcast.11), custom_call_target="tpu_custom_call" | custom-call | flops 603979776 | bytes 3145728 | tf_op jit(solution)/shard_map/pallas_call | solution.py:213
  49.6 0.7 %copy.11 = f32[1,512,128]{2,1,0:T(8,128)} copy(f32[1,512,128]{2,1,0:T(8,128)S(1)} %bitcast.13) | data formatting | bytes 524288
  50.3 0.7 %copy.12 = f32[512,1,128]{2,1,0:T(1,128)} copy(f32[512,1,128]{2,1,0:T(1,128)S(1)} %bitcast.12) | data formatting | bytes 524288
Async XLA Ops:
  0.6 1.4 %copy-start = (bf16[1,1,48,128,128]{4,3,2,1,0:T(8,128)(2,1)S(1)}, bf16[1,1,48,128,128]{4,3,2,1,0:T(8,128)(2,1)}, u32[]{:S(2)}) copy-start(bf16[1,1,48,128,128]{4,3,2,1,0:T(8,128)(2,1)} %param.10) | copy-start | bytes 4718596
  2.0 1.4 %copy-start.1 = (bf16[1,1,48,128,128]{4,3,2,1,0:T(8,128)(2,1)S(1)}, bf16[1,1,48,128,128]{4,3,2,1,0:T(8,128)(2,1)}, u32[]{:S(2)}) copy-start(bf16[1,1,48,128,128]{4,3,2,1,0:T(8,128)(2,1)} %param.11) | copy-start | bytes 4718596
  3.4 0.9 %copy-start.2 = (f32[1,512,128]{2,1,0:T(8,128)S(1)}, f32[1,512,128]{2,1,0:T(8,128)}, u32[]{:S(2)}) copy-start(f32[1,512,128]{2,1,0:T(8,128)} %param.6) | copy-start | bytes 786436
  4.4 0.9 %copy-start.3 = (f32[512,1,128]{2,1,0:T(1,128)S(1)}, f32[512,1,128]{2,1,0:T(1,128)}, u32[]{:S(2)}) copy-start(f32[512,1,128]{2,1,0:T(1,128)} %param.7) | copy-start | bytes 786436
  5.3 0.7 %copy-start.4 = (s32[1,1,48]{2,1,0:T(1,128)S(1)}, s32[1,1,48]{2,1,0:T(1,128)}, u32[]{:S(2)}) copy-start(s32[1,1,48]{2,1,0:T(1,128)} %param.8) | copy-start | bytes 580
  6.0 0.7 %copy-start.5 = (s32[1,1,48]{2,1,0:T(1,128)S(1)}, s32[1,1,48]{2,1,0:T(1,128)}, u32[]{:S(2)}) copy-start(s32[1,1,48]{2,1,0:T(1,128)} %param.9) | copy-start | bytes 580

commit v2 on v1

--- a/solution.py
+++ b/solution.py
@@ -8,6 +8,7 @@
 from jax.sharding import PartitionSpec as P
 
 BS = 128
+GROUP = 8
 MESH = pl.DeviceIdType.MESH
 NT = (((1,), (1,)), ((), ()))
 NN = (((1,), (0,)), ((), ()))
@@ -60,28 +61,38 @@
     return tile
 
 
-def pack(seg_ref, wseg_ref, tab, line, index, own, out_ref, place, turn_ref):
+def weight_sums(ref, place, own):
+    both = ref[place, own : own + 16, :].astype(jnp.float32)
+    return both[0:8] + both[8:16]
+
+
+def pack(seg_ref, wseg_ref, tab, line, index, own, out_ref, place, turn_ref, held_ref=None, held=None):
     pieces = spots(index, own)
     slots = [tab[line, block] for block, _, _ in pieces]
     for k, (slot, (_, first, rows)) in enumerate(zip(slots, pieces)):
-        out_ref[place, k * BS : k * BS + rows, :] = part(seg_ref[slot], first, rows, turn_ref).astype(jnp.bfloat16)
+        at = slice(k * BS, k * BS + rows)
+        sums = part(seg_ref[slot], first, rows, turn_ref)
+        if held_ref is not None:
+            sums = sums + held_ref[held, at, :].astype(jnp.float32)
+        out_ref[place, at, :] = sums.astype(jnp.bfloat16)
     tile = weight_tile(wseg_ref, slots)
+    if held_ref is not None:
+        tile = tile + weight_sums(held_ref, held, own)
     high = tile.astype(jnp.bfloat16).astype(jnp.float32)
     both = jnp.concatenate([high, tile - high], axis=0)
     out_ref[place, own : own + 16, :] = both.astype(jnp.bfloat16)
 
 
-def update(old_ref, seg_ref, wseg_ref, tab, line, index, own, recv_ref, waits, acc_ref, turn_ref, new_ref):
+def update(old_ref, seg_ref, wseg_ref, tab, line, index, own, terms, acc_ref, turn_ref, new_ref):
     pieces = spots(index, own)
     slots = [tab[line, block] for block, _, _ in pieces]
     for k, (slot, (_, first, rows)) in enumerate(zip(slots, pieces)):
         acc_ref[k * BS : k * BS + rows, :] = part(seg_ref[slot], first, rows, turn_ref)
     tile = weight_tile(wseg_ref, slots)
-    for place, wait in enumerate(waits):
+    for wait, recv_ref, place in terms:
         wait()
         acc_ref[...] += recv_ref[place, 0:own, :].astype(jnp.float32)
-        both = recv_ref[place, own : own + 16, :].astype(jnp.float32)
-        tile = tile + (both[0:8] + both[8:16])
+        tile = tile + weight_sums(recv_ref, place, own)
     for k, (_, first, rows) in enumerate(pieces):
         turned = jnp.broadcast_to(tile[k : k + 1, :], (BS, BS)).T
         turned = part(turned, first, rows, turn_ref)
@@ -92,29 +103,39 @@
 
 def kernel(
     n_row, n_col, count, own_u, own_i,
-    users, items, bu, bi, ratings, weights,
+    users_hbm, items_hbm, bu_hbm, bi_hbm, ratings, weights,
     new_users, new_items,
+    users, items, bu, bi,
     slab_u, slab_i, rat, wts, resid, seg_u, seg_i, wseg_u, wseg_i,
-    send_u, send_i, recv_u, recv_i, acc_u, acc_i, turn, pad, tab_v, tab,
-    load_sem, gu_send, gu_recv, gi_send, gi_recv, ru_send, ru_recv, ri_send, ri_recv,
+    send_u, send_t, send_i, recv_u, recv_t, recv_i, acc_u, acc_i, turn, pad, tab_v, tab,
+    load_sem, gu_send, gu_recv, gi_send, gi_recv, gf_send, gf_recv,
+    ru_send, ru_recv, rt_send, rt_recv, ri_send, ri_recv,
 ):
     row, col = lax.axis_index("row"), lax.axis_index("col")
     col_peers = [lax.rem(col + d, n_col) for d in range(1, n_col)]
-    row_peers = [lax.rem(row + d, n_row) for d in range(1, n_row)]
+    twin = row + 1 - 2 * lax.rem(row, 2)
+    half = n_row // 2
+    row_peers = [lax.rem(row + 2 * d, n_row) for d in range(1, half)]
 
     barrier = pltpu.get_barrier_semaphore()
     for peer in col_peers:
         pl.semaphore_signal(barrier, inc=1, device_id=(row, peer), device_id_type=MESH)
-    for peer in row_peers:
+    for peer in row_peers + [twin]:
         pl.semaphore_signal(barrier, inc=1, device_id=(peer, col), device_id_type=MESH)
-    load_rat = pltpu.make_async_copy(ratings, rat, load_sem.at[0])
-    load_wts = pltpu.make_async_copy(weights, wts, load_sem.at[1])
-    load_rat.start()
-    load_wts.start()
+    sources = (users_hbm, items_hbm, bu_hbm, bi_hbm, weights, ratings)
+    loads = [
+        pltpu.make_async_copy(source, place, load_sem.at[k])
+        for k, (source, place) in enumerate(zip(sources, (users, items, bu, bi, wts, rat)))
+    ]
+    for load in loads:
+        load.start()
+    load_wts, load_rat = loads[4:]
+    for load in loads[:4]:
+        load.wait()
     mine_u, mine_i = owned(slab_u, col, own_u), owned(slab_i, row, own_i)
     mine_u[...] = users[...].astype(jnp.bfloat16).reshape(mine_u.shape)
     mine_i[...] = items[...].astype(jnp.bfloat16).reshape(mine_i.shape)
-    pl.semaphore_wait(barrier, n_col + n_row - 2)
+    pl.semaphore_wait(barrier, n_col + half - 1)
 
     gathers = []
     for place, peer in enumerate(col_peers):
@@ -122,7 +143,7 @@
             src_ref=mine_u, dst_ref=mine_u,
             send_sem=gu_send.at[place], recv_sem=gu_recv.at[place],
             device_id=(row, peer), device_id_type=MESH))
-    for place, peer in enumerate(row_peers):
+    for place, peer in enumerate(row_peers + [twin]):
         gathers.append(pltpu.make_async_remote_copy(
             src_ref=mine_i, dst_ref=mine_i,
             send_sem=gi_send.at[place], recv_sem=gi_recv.at[place],
@@ -134,14 +155,13 @@
     prev_i, last_i, key_i = chain_tables(bi, pad, count)
     for line, values in enumerate((prev_u, prev_i, last_u, last_i, key_u, key_i)):
         tab_v[line : line + 1, :] = values
-    to_scalar = pltpu.make_async_copy(tab_v, tab, load_sem.at[2])
+    to_scalar = pltpu.make_async_copy(tab_v, tab, load_sem.at[6])
     to_scalar.start()
     seg_u[0] = jnp.zeros((BS, BS), jnp.float32)
     seg_i[0] = jnp.zeros((BS, BS), jnp.float32)
     wseg_u[0] = jnp.zeros((8, BS), jnp.float32)
     wseg_i[0] = jnp.zeros((8, BS), jnp.float32)
     to_scalar.wait()
-    load_rat.wait()
     load_wts.wait()
 
     ones = jnp.ones((8, BS), jnp.bfloat16)
@@ -154,19 +174,42 @@
 
     lax.fori_loop(0, count, weight_step, 0, unroll=4)
 
-    for copy in gathers:
+    load_rat.wait()
+    forwards = []
+    for place in range(half - 1):
+        gathers[n_col - 1 + place].wait_recv()
+        block = owned(slab_i, lax.rem(row + n_row - 2 * (place + 1), n_row), own_i)
+        copy = pltpu.make_async_remote_copy(
+            src_ref=block, dst_ref=block, send_sem=gf_send.at[place], recv_sem=gf_recv.at[place],
+            device_id=(twin, col), device_id_type=MESH)
+        copy.start()
+        forwards.append(copy)
+    for k, copy in enumerate(gathers):
+        copy.wait_send()
+        if k < n_col - 1 or k == len(gathers) - 1:
+            copy.wait_recv()
+    for copy in forwards:
         copy.wait()
 
-    def user_step(b, carry):
-        u = slab_u[tab[4, b]]
-        v = slab_i[tab[5, b]]
-        pred = dot(u, v, NT)
-        r = (wts[b].astype(jnp.float32) * (pred - rat[b].astype(jnp.float32))).astype(jnp.bfloat16)
-        resid[b] = r
-        seg_u[b + 1] = seg_u[tab[0, b]] + dot(r, v, NN)
+    group = GROUP if count % GROUP == 0 else 1
+
+    def user_step(g, carry):
+        blocks = [g * group + k for k in range(group)]
+        us = [slab_u[tab[4, b]] for b in blocks]
+        vs = [slab_i[tab[5, b]] for b in blocks]
+        preds = [dot(u, v, NT) for u, v in zip(us, vs)]
+        rs = [
+            (wts[b].astype(jnp.float32) * (pred - rat[b].astype(jnp.float32))).astype(jnp.bfloat16)
+            for b, pred in zip(blocks, preds)
+        ]
+        grads = [dot(r, v, NN) for r, v in zip(rs, vs)]
+        for b, r in zip(blocks, rs):
+            resid[b] = r
+        for b, grad in zip(blocks, grads):
+            seg_u[b + 1] = seg_u[tab[0, b]] + grad
         return carry
 
-    lax.fori_loop(0, count, user_step, 0, unroll=4)
+    lax.fori_loop(0, count // group, user_step, 0)
 
     sends_u = []
     for place, peer in enumerate(col_peers):
@@ -185,9 +228,20 @@
 
     lax.fori_loop(0, count, item_step, 0, unroll=4)
 
+    to_twin = []
+    for place in list(range(1, half)) + [0]:
+        pack(seg_i, wseg_i, tab, 3, lax.rem(twin + 2 * place, n_row), own_i, send_t, place, turn)
+        copy = pltpu.make_async_remote_copy(
+            src_ref=send_t.at[place], dst_ref=recv_t.at[place],
+            send_sem=rt_send.at[place], recv_sem=rt_recv.at[place],
+            device_id=(twin, col), device_id_type=MESH)
+        copy.start()
+        to_twin.append(copy)
+
     sends_i = []
     for place, peer in enumerate(row_peers):
-        pack(seg_i, wseg_i, tab, 3, peer, own_i, send_i, place, turn)
+        to_twin[place].wait_recv()
+        pack(seg_i, wseg_i, tab, 3, peer, own_i, send_i, place, turn, recv_t, place + 1)
         copy = pltpu.make_async_remote_copy(
             src_ref=send_i.at[place], dst_ref=recv_i.at[place],
             send_sem=ri_send.at[place], recv_sem=ri_recv.at[place],
@@ -195,9 +249,11 @@
         copy.start()
         sends_i.append(copy)
 
-    update(users, seg_u, wseg_u, tab, 2, col, own_u, recv_u, [c.wait_recv for c in sends_u], acc_u, turn, new_users)
-    update(items, seg_i, wseg_i, tab, 3, row, own_i, recv_i, [c.wait_recv for c in sends_i], acc_i, turn, new_items)
-    for copy in sends_u + sends_i:
+    terms_u = [(c.wait_recv, recv_u, k) for k, c in enumerate(sends_u)]
+    terms_i = [(to_twin[-1].wait_recv, recv_t, 0)] + [(c.wait_recv, recv_i, k) for k, c in enumerate(sends_i)]
+    update(users, seg_u, wseg_u, tab, 2, col, own_u, terms_u, acc_u, turn, new_users)
+    update(items, seg_i, wseg_i, tab, 3, row, own_i, terms_i, acc_i, turn, new_items)
+    for copy in sends_u + to_twin + sends_i:
         copy.wait_send()
 
 
@@ -205,6 +261,7 @@
     own_u, own_i = users.shape[1], items.shape[0]
     width = users.shape[2]
     count = block_user.shape[2]
+    half = n_row // 2
     all_u, all_i = own_u * n_col, own_i * n_row
     vmem = pl.BlockSpec(memory_space=pltpu.VMEM)
     hbm = pl.BlockSpec(memory_space=pl.ANY)
@@ -216,9 +273,13 @@
             jax.ShapeDtypeStruct((own_u, width), f32),
             jax.ShapeDtypeStruct((own_i, width), f32),
         ),
-        in_specs=[vmem, vmem, vmem, vmem, hbm, hbm],
+        in_specs=[hbm] * 6,
         out_specs=(vmem, vmem),
         scratch_shapes=[
+            pltpu.VMEM((own_u, width), f32),
+            pltpu.VMEM((own_i, width), f32),
+            pltpu.VMEM((1, count), i32),
+            pltpu.VMEM((1, count), i32),
             pltpu.VMEM((all_u // BS, BS, width), bf16),
             pltpu.VMEM((all_i // BS, BS, width), bf16),
             pltpu.VMEM((count, BS, BS), bf16),
@@ -229,27 +290,33 @@
             pltpu.VMEM((count + 1, 8, BS), f32),
             pltpu.VMEM((count + 1, 8, BS), f32),
             pltpu.VMEM((n_col - 1, own_u + 16, width), bf16),
-            pltpu.VMEM((n_row - 1, own_i + 16, width), bf16),
+            pltpu.VMEM((half, own_i + 16, width), bf16),
+            pltpu.VMEM((half - 1, own_i + 16, width), bf16),
             pltpu.VMEM((n_col - 1, own_u + 16, width), bf16),
-            pltpu.VMEM((n_row - 1, own_i + 16, width), bf16),
+            pltpu.VMEM((half, own_i + 16, width), bf16),
+            pltpu.VMEM((half - 1, own_i + 16, width), bf16),
             pltpu.VMEM((own_u, width), f32),
             pltpu.VMEM((own_i, width), f32),
             pltpu.VMEM((BS, BS), f32),
             pltpu.VMEM((8, 128), i32),
             pltpu.VMEM((8, 128), i32),
             pltpu.SMEM((8, 128), i32),
-            dma((3,)),
+            dma((7,)),
             dma((n_col - 1,)),
             dma((n_col - 1,)),
-            dma((n_row - 1,)),
-            dma((n_row - 1,)),
+            dma((half,)),
+            dma((half,)),
+            dma((half - 1,)),
+            dma((half - 1,)),
             dma((n_col - 1,)),
             dma((n_col - 1,)),
-            dma((n_row - 1,)),
-            dma((n_row - 1,)),
+            dma((half,)),
+            dma((half,)),
+            dma((half - 1,)),
+            dma((half - 1,)),
         ],
         compiler_params=pltpu.CompilerParams(
-            collective_id=0, has_side_effects=True, vmem_limit_bytes=40 << 20
+            collective_id=0, has_side_effects=True, vmem_limit_bytes=60 << 20
         ),
         cost_estimate=pl.CostEstimate(
             flops=6 * count * BS * BS * width, bytes_accessed=4 * count * BS * BS, transcendentals=0

time: 51.3 us -> 36.3 us (0.71)
  the two profiles are of different devices: /device:TPU:1 before, /device:TPU:0 now
where the time goes in v2:
time: 36.3 us; the launch traced here: 36.1 us
  Pallas kernels  32.1 us (88%)
  local copies, waits for them, and re-layouts  3.34 us (9%)
  between operations  0.64 us (2%)
    pallas_call x1, Pallas kernels, shards(): pl.pallas_call(functools.partial(kernel, n_row, n_col, count, own_u, own_...  32.1 us
    unnamed x2, local copies, waits for them, and re-layouts  3.34 us

profile of v2, /device:TPU:0, one launch (start us, length us, event | category | flops | bytes accessed | tf_op | source)
XLA Modules:
  0.0 36.1 jit_solution(15293542102524303333)
XLA Ops:
  0.6 32.1 %shard_map.77 = (f32[512,128]{1,0:T(8,128)}, f32[512,128]{1,0:T(8,128)}) custom-call(f32[512,128]{1,0:T(8,128)} %bitcast.14, f32[512,128]{1,0:T(8,128)} %bitcast.15, s32[1,48]{1,0:T(1,128)} %bitcast.16, s32[1,48]{1,0:T(1,128)} %bitcast.17, bf16[48,128,128]{2,1,0:T(8,128)(2,1)} %bitcast.10, bf16[48,128,128]{2,1,0:T(8,128)(2,1)} %bitcast.11), custom_call_target="tpu_custom_call" | custom-call | flops 603979776 | bytes 3145728 | tf_op jit(solution)/shard_map/pallas_call | solution.py:270
  32.8 1.7 %copy.11 = f32[1,512,128]{2,1,0:T(8,128)} copy(f32[1,512,128]{2,1,0:T(8,128)} %bitcast.13) | data formatting | bytes 524288
  34.4 1.7 %copy.12 = f32[512,1,128]{2,1,0:T(1,128)} copy(f32[512,1,128]{2,1,0:T(1,128)} %bitcast.12) | data formatting | bytes 524288

commit v3 on v2

--- a/solution.py
+++ b/solution.py
@@ -8,7 +8,7 @@
 from jax.sharding import PartitionSpec as P
 
 BS = 128
-GROUP = 8
+GROUP = 16
 MESH = pl.DeviceIdType.MESH
 NT = (((1,), (1,)), ((), ()))
 NN = (((1,), (0,)), ((), ()))
@@ -221,12 +221,14 @@
         copy.start()
         sends_u.append(copy)
 
-    def item_step(b, carry):
-        u = slab_u[tab[4, b]]
-        seg_i[b + 1] = seg_i[tab[1, b]] + dot(resid[b], u, TN)
+    def item_step(g, carry):
+        blocks = [g * group + k for k in range(group)]
+        grads = [dot(resid[b], slab_u[tab[4, b]], TN) for b in blocks]
+        for b, grad in zip(blocks, grads):
+            seg_i[b + 1] = seg_i[tab[1, b]] + grad
         return carry
 
-    lax.fori_loop(0, count, item_step, 0, unroll=4)
+    lax.fori_loop(0, count // group, item_step, 0)
 
     to_twin = []
     for place in list(range(1, half)) + [0]:
@@ -264,14 +266,14 @@
     half = n_row // 2
     all_u, all_i = own_u * n_col, own_i * n_row
     vmem = pl.BlockSpec(memory_space=pltpu.VMEM)
-    hbm = pl.BlockSpec(memory_space=pl.ANY)
+    hbm = pl.BlockSpec(memory_space=pltpu.HBM)
     bf16, f32, i32 = jnp.bfloat16, jnp.float32, jnp.int32
     dma = pltpu.SemaphoreType.DMA
     new_users, new_items = pl.pallas_call(
         functools.partial(kernel, n_row, n_col, count, own_u, own_i),
         out_shape=(
-            jax.ShapeDtypeStruct((own_u, width), f32),
-            jax.ShapeDtypeStruct((own_i, width), f32),
+            pltpu.VMEM((own_u, width), f32),
+            pltpu.VMEM((own_i, width), f32),
         ),
         in_specs=[hbm] * 6,
         out_specs=(vmem, vmem),

time: 36.3 us -> 32.9 us (0.906)
  local copies, waits for them, and re-layouts: 3.34 us -> 1.41 us
  Pallas kernels: 32.1 us -> 30.7 us
    unnamed x2, local copies, waits for them, and re-layouts: 3.34 us -> 1.41 us
    pallas_call x1, Pallas kernels: 32.1 us -> 30.7 us  [shards(): pl.pallas_call(functools.partial(kernel, n_row, n_col, count, own_u, own_...]
where the time goes in v3:
time: 32.9 us; the launch traced here: 32.8 us
  Pallas kernels  30.7 us (93%)
  local copies, waits for them, and re-layouts  1.41 us (4%)
  between operations  0.64 us (2%)
    pallas_call x1, Pallas kernels, shards(): pl.pallas_call(functools.partial(kernel, n_row, n_col, count, own_u, own_...  30.7 us
    unnamed x2, local copies, waits for them, and re-layouts  1.41 us

profile of v3, /device:TPU:0, one launch (start us, length us, event | category | flops | bytes accessed | tf_op | source)
XLA Modules:
  0.0 32.8 jit_solution(1773531926732697091)
XLA Ops:
  0.6 30.7 %shard_map.77 = (f32[512,128]{1,0:T(8,128)S(1)}, f32[512,128]{1,0:T(8,128)S(1)}) custom-call(f32[512,128]{1,0:T(8,128)} %bitcast.14, f32[512,128]{1,0:T(8,128)} %bitcast.15, s32[1,48]{1,0:T(1,128)} %bitcast.16, s32[1,48]{1,0:T(1,128)} %bitcast.17, bf16[48,128,128]{2,1,0:T(8,128)(2,1)} %bitcast.12, bf16[48,128,128]{2,1,0:T(8,128)(2,1)} %bitcast.13), custom_call_target="tpu_custom_call" | custom-call | flops 603979776 | bytes 3145728 | tf_op jit(solution)/shard_map/pallas_call | solution.py:272
  31.4 0.7 %copy.11 = f32[1,512,128]{2,1,0:T(8,128)} copy(f32[1,512,128]{2,1,0:T(8,128)S(1)} %bitcast.11) | data formatting | bytes 524288
  32.1 0.7 %copy.12 = f32[512,1,128]{2,1,0:T(1,128)} copy(f32[512,1,128]{2,1,0:T(1,128)S(1)} %bitcast.10) | data formatting | bytes 524288

commit v4 on v3

--- a/solution.py
+++ b/solution.py
@@ -8,7 +8,7 @@
 from jax.sharding import PartitionSpec as P
 
 BS = 128
-GROUP = 16
+GROUP = 24
 MESH = pl.DeviceIdType.MESH
 NT = (((1,), (1,)), ((), ()))
 NN = (((1,), (0,)), ((), ()))
@@ -148,7 +148,7 @@
             src_ref=mine_i, dst_ref=mine_i,
             send_sem=gi_send.at[place], recv_sem=gi_recv.at[place],
             device_id=(peer, col), device_id_type=MESH))
-    for copy in gathers:
+    for copy in gathers[n_col - 1:][::-1] + gathers[:n_col - 1][::-1]:
         copy.start()
 
     prev_u, last_u, key_u = chain_tables(bu, pad, count)

time: 32.9 us -> 31.8 us (0.967); the launches traced: 32.8 us -> 31.2 us
  Pallas kernels: 30.7 us -> 29.2 us
    pallas_call x1, Pallas kernels: 30.7 us -> 29.2 us  [shards(): pl.pallas_call(functools.partial(kernel, n_row, n_col, count, own_u, own_...]
where the time goes in v4:
time: 31.8 us; the launch traced here: 31.2 us
  Pallas kernels  29.2 us (92%)
  local copies, waits for them, and re-layouts  1.41 us (4%)
  between operations  0.64 us (2%)
    pallas_call x1, Pallas kernels, shards(): pl.pallas_call(functools.partial(kernel, n_row, n_col, count, own_u, own_...  29.2 us
    unnamed x2, local copies, waits for them, and re-layouts  1.41 us

profile of v4, /device:TPU:0, one launch (start us, length us, event | category | flops | bytes accessed | tf_op | source)
XLA Modules:
  0.0 31.2 jit_solution(1721622098826193947)
XLA Ops:
  0.6 29.2 %shard_map.77 = (f32[512,128]{1,0:T(8,128)S(1)}, f32[512,128]{1,0:T(8,128)S(1)}) custom-call(f32[512,128]{1,0:T(8,128)} %bitcast.14, f32[512,128]{1,0:T(8,128)} %bitcast.15, s32[1,48]{1,0:T(1,128)} %bitcast.16, s32[1,48]{1,0:T(1,128)} %bitcast.17, bf16[48,128,128]{2,1,0:T(8,128)(2,1)} %bitcast.12, bf16[48,128,128]{2,1,0:T(8,128)(2,1)} %bitcast.13), custom_call_target="tpu_custom_call" | custom-call | flops 603979776 | bytes 3145728 | tf_op jit(solution)/shard_map/pallas_call | solution.py:272
  29.8 0.7 %copy.11 = f32[1,512,128]{2,1,0:T(8,128)} copy(f32[1,512,128]{2,1,0:T(8,128)S(1)} %bitcast.11) | data formatting | bytes 524288
  30.5 0.7 %copy.12 = f32[512,1,128]{2,1,0:T(1,128)} copy(f32[512,1,128]{2,1,0:T(1,128)S(1)} %bitcast.10) | data formatting | bytes 524288
